TPU v7x, 32 devices: a whole 2x2x4 slice. The times are simulated.
32 devices in a mesh: flow: 8 (over z, y), grp: 4 (over x, core).
Axes of the slice: x: 2, y: 2, z: 4, core: 2. Of those that a mesh axis runs over, the one named last changes fastest.
Arguments:
- velocity: float32 [3, 64, 128, 256], P(None, 'flow', 'grp'), may hold values from -6 to 6
- eddy_visc: float32 [64, 128, 256], P('flow', 'grp'), may hold values from 0.05 to 0.4
- projection: bfloat16 [125, 512], replicated, may hold values from -0.25 to 0.25
- acoustic_state: float32 [4, 125, 4096], P(None, None, ('flow', 'grp')), may hold values from -6 to 6
- route_send: int32 [32, 32, 4], P(('flow', 'grp')), may hold values from 0 to 127, as said below
- route_place: int32 [32, 128], P(('flow', 'grp')), may hold values from 0 to 127, as said below
Outputs:
- velocity_out: float32 [3, 64, 128, 256], P(None, 'flow', 'grp')
- acoustic_out: float32 [4, 125, 4096], P(None, None, ('flow', 'grp'))
Inputs may be any that keep to these rules, and one draw needn't show every extreme that they name: `route_send`: row h lists, for each owner o, the local indices of home h's elements that o holds in 4 slots, -1 in an empty slot; every local element of h stands exactly once in row h; an owner holds elements of 32 home devices, all 4 slots of each filled. `route_place`: row o is a permutation of the filled slots h * 4 + k of owner o; position j of owner o holds home h's element route_send[h, o, k].
All inputs are finite; a program needn't handle non-finite values.
Results may differ from a plain program's by a relative error of at most 0.0003.
Values sent between devices are 32-bit elements; how exact they have to be, the bound alone decides.
A program may use at most 64 MiB of HBM per device.

v0:
```python
import functools
import math

import jax
import jax.numpy as jnp
import ml_dtypes
import numpy as np
from jax import lax
from jax.experimental import pallas as pl
from jax.experimental.pallas import tpu as pltpu
from jax.sharding import PartitionSpec as P

LES_SECTIONS = 2
AC_SECTIONS = 2

TIME_STEP_LES = 0.15
TIME_STEP_ACOUSTIC = 0.02
GEOMETRY = 2.0
LIFT_FACTOR = 20.0
F32 = jnp.float32
BF16 = jnp.bfloat16


def gll_derivative():
    gll_nodes = np.array([-1.0, -math.sqrt(3.0 / 7.0), 0.0, math.sqrt(3.0 / 7.0), 1.0])
    bary_weights = np.array(
        [
            1.0
            / np.prod([gll_nodes[first] - gll_nodes[other] for other in range(5) if other != first])
            for first in range(5)
        ]
    )
    matrix = np.zeros((5, 5))
    for row_id in range(5):
        for col_id in range(5):
            if row_id != col_id:
                matrix[row_id, col_id] = (
                    bary_weights[col_id]
                    / bary_weights[row_id]
                    / (gll_nodes[row_id] - gll_nodes[col_id])
                )
    for row_id in range(5):
        matrix[row_id, row_id] = -matrix[row_id].sum()
    return matrix


def operators():
    dmat = gll_derivative()
    eye = np.eye(5)
    kron = lambda a, b, c: np.kron(np.kron(a, b), c)
    derivs = [kron(dmat, eye, eye), kron(eye, dmat, eye), kron(eye, eye, dmat)]
    own = np.zeros((512, 512))
    for k in range(3):
        u = 128 * (k + 1)
        own[u : u + 125, 0:125] += -GEOMETRY * derivs[k].T
        own[0:125, u : u + 125] += -GEOMETRY * derivs[k].T
    half = 0.5 * LIFT_FACTOR
    send = np.zeros((512, 768))
    take = np.zeros((768, 512))
    for d in range(3):
        pos = [np.arange(125) // 25, np.arange(125) // 5 % 5, np.arange(125) % 5][d]
        others = [k for k in range(3) if k != d]
        faces = {-1: np.where(pos == 0)[0], 1: np.where(pos == 4)[0]}
        for sign in (-1, 1):
            for n in faces[sign]:
                own[128 * (d + 1) + n, n] += half * sign
                own[n, 128 * (d + 1) + n] += half * sign
                for c in range(4):
                    own[128 * c + n, 128 * c + n] -= half
            base = (2 * d + (sign + 1) // 2) * 128
            for i, n in enumerate(faces[sign]):
                send[n, base + i] = 1.0
                send[128 * (d + 1) + n, base + i] = sign
                for t, k in enumerate(others):
                    send[128 * (k + 1) + n, base + 25 * (t + 1) + i] = 1.0
            for i, n in enumerate(faces[sign]):
                take[base + i, n] = 1.0
                take[base + i, 128 * (d + 1) + n] = -sign
                for t, k in enumerate(others):
                    take[base + 25 * (t + 1) + i, 128 * (k + 1) + n] = 1.0
    own = own * TIME_STEP_ACOUSTIC
    high = own.astype(ml_dtypes.bfloat16)
    low = (own - high.astype(np.float64)).astype(ml_dtypes.bfloat16)
    return high, low, send.astype(ml_dtypes.bfloat16), take.astype(ml_dtypes.bfloat16)


def cell_order(by, bz):
    count = by * bz * 8
    ids = np.arange(count)
    matrix = np.zeros((count, count), ml_dtypes.bfloat16)
    matrix[ids, (ids % 8) * (by * bz) + ids // 8] = 1
    return matrix


def pieces(value, count):
    out = []
    for _ in range(count):
        part = value.astype(BF16)
        out.append(part)
        value = value - part.astype(F32)
    return out


def mm(a, b):
    return jnp.dot(a, b, preferred_element_type=F32)


def pick(onehot, value):
    a, b, c = pieces(value, 3)
    return (mm(onehot, a) + mm(onehot, b)) + mm(onehot, c)


def outgoing_rows(state_ref, place_ref, wide_ref, slots):
    count = place_ref.shape[1]
    wide_ref[...] = jnp.zeros_like(wide_ref)
    for c in range(4):
        wide_ref[c, 0:125, :] = state_ref[c]
    rows = jnp.concatenate([wide_ref[c].T for c in range(4)], axis=1)
    ids = lax.broadcasted_iota(jnp.int32, (slots, count), 0)
    onehot = jnp.where(ids == place_ref[...], 1.0, 0.0).astype(BF16)
    return pick(onehot, rows)


def home_rows(arrived, send_ref, count):
    slots = send_ref.shape[1]
    ids = lax.broadcasted_iota(jnp.int32, (count, slots), 0)
    onehot = jnp.where(ids == send_ref[...], 1.0, 0.0).astype(BF16)
    return pick(onehot, arrived)


def leaving_rows(state, send_ref):
    slots = send_ref.shape[1]
    count = state.shape[0]
    ids = lax.broadcasted_iota(jnp.int32, (count, slots), 0)
    onehot = jnp.where(ids == send_ref[...], 1.0, 0.0).T.astype(BF16)
    return pick(onehot, state)


def place_out(returned, place_ref, out_ref):
    slots = returned.shape[0]
    count = place_ref.shape[1]
    ids = lax.broadcasted_iota(jnp.int32, (slots, count), 0)
    onehot = jnp.where(ids == place_ref[...], 1.0, 0.0).T.astype(BF16)
    rows = pick(onehot, returned)
    for c in range(4):
        out_ref[c] = rows[:, 128 * c : 128 * (c + 1)].T[0:125]


def faces_out(state, send_mat_ref):
    high, low = pieces(state, 2)
    mat = send_mat_ref[...]
    return mm(high, mat) + mm(low, mat)


def advance(state, faces, x_low, x_high, y_low, y_high, source, own_ref, own_low_ref, take_ref, bz):
    count = state.shape[0]
    rows = lax.broadcasted_iota(jnp.int32, (count, 128), 0)
    part = lambda i: faces[:, 128 * i : 128 * (i + 1)]
    from_low_y = jnp.concatenate([y_low, part(3)[: count - bz]], axis=0)
    from_high_y = jnp.concatenate([part(2)[bz:], y_high], axis=0)
    from_low_z = jnp.where(rows % bz == 0, 0.0, pltpu.roll(part(5), 1, 0))
    from_high_z = jnp.where(rows % bz == bz - 1, 0.0, pltpu.roll(part(4), count - 1, 0))
    incoming = jnp.concatenate(
        [x_low, x_high, from_low_y, from_high_y, from_low_z, from_high_z], axis=1
    )
    high, low = pieces(state, 2)
    mat = own_ref[...]
    change = mm(high, mat) + (mm(high, own_low_ref[...]) + mm(low, mat))
    in_high, in_low = pieces(incoming, 2)
    lift = mm(in_high, take_ref[...]) + mm(in_low, take_ref[...])
    scale = TIME_STEP_ACOUSTIC * 0.5 * LIFT_FACTOR
    return state + (change + scale * lift) - TIME_STEP_ACOUSTIC * source


def les_plane(vel, visc):
    rows, lanes = visc[1].shape
    lane = lax.broadcasted_iota(jnp.int32, (rows, lanes), 1)

    def around(field):
        mid = field[1]
        return (
            field[0],
            field[2],
            pltpu.roll(mid, 1, 0),
            pltpu.roll(mid, rows - 1, 0),
            jnp.where(lane == 0, 0.0, pltpu.roll(mid, 1, 1)),
            jnp.where(lane == lanes - 1, 0.0, pltpu.roll(mid, lanes - 1, 1)),
        )

    weights = [0.5 * (visc[1] + w) for w in around(visc)]
    mids = [f[1] for f in vel]
    near = [around(f) for f in vel]
    d = lambda c, axis: 0.5 * (near[c][2 * axis + 1] - near[c][2 * axis])
    vort_x = d(2, 1) - d(1, 2)
    vort_y = d(0, 2) - d(2, 0)
    vort_z = d(1, 0) - d(0, 1)
    lamb = [
        vort_y * mids[2] - vort_z * mids[1],
        vort_z * mids[0] - vort_x * mids[2],
        vort_x * mids[1] - vort_y * mids[0],
    ]
    new = []
    for c in range(3):
        total = weights[0] * (near[c][0] - mids[c])
        for i in range(1, 6):
            total = total + weights[i] * (near[c][i] - mids[c])
        new.append(mids[c] + TIME_STEP_LES * (total - lamb[c]))
    return new, lamb


def les_sections(ext_ref, mid_ref, cells_ref, vel_out_ref, edges):
    planes = ext_ref.shape[1]
    rows, lanes = ext_ref.shape[2:]
    own_rows = vel_out_ref.shape[2]
    at_x0, at_x1, at_y0, at_y1 = edges
    row = lax.broadcasted_iota(jnp.int32, (rows, lanes), 0)
    below = jnp.where(at_y0, own_rows + 4, rows)
    above = jnp.where(at_y1, own_rows, own_rows + 4)
    inside = jnp.logical_or(
        row < above, jnp.logical_and(row >= own_rows + 4, row < below)
    ).astype(F32)

    def first(i, carry):
        vel = [[ext_ref[c, i + j] for j in range(3)] for c in range(3)]
        visc = [ext_ref[3, i + j] for j in range(3)]
        new, _ = les_plane(vel, visc)
        outside = jnp.logical_or(
            jnp.logical_and(at_x0, i == 0), jnp.logical_and(at_x1, i == planes - 3)
        )
        keep = inside * jnp.where(outside, 0.0, 1.0)
        for c in range(3):
            mid_ref[c, i] = new[c] * keep
        return carry

    lax.fori_loop(0, planes - 2, first, 0)

    def second(i, carry):
        vel = [[mid_ref[c, i + j] for j in range(3)] for c in range(3)]
        visc = [ext_ref[3, i + 1 + j] for j in range(3)]
        new, lamb = les_plane(vel, visc)
        at = pl.ds(pl.multiple_of(i * 8, 8), 8)
        for c in range(3):
            vel_out_ref[c, i] = new[c][0:own_rows]
            for ey in range(own_rows // 8):
                cells_ref[c, at, ey * lanes : (ey + 1) * lanes] = lamb[c][8 * ey : 8 * ey + 8]
        return carry

    lax.fori_loop(0, planes - 4, second, 0)


def source_rows(cells_ref, order_ref, proj_ref):
    count = order_ref.shape[0] // 8
    parts = [jnp.zeros((count, 128), F32)]
    for c in range(3):
        moved = mm(cells_ref[c].astype(BF16), order_ref[...]).astype(BF16)
        cells = jnp.concatenate([moved[:, count * k : count * (k + 1)] for k in range(8)], axis=0)
        parts.append(mm(proj_ref[...], cells).T)
    return jnp.concatenate(parts, axis=1)


def pre_kernel(slots, state_ref, place_ref, out_ref, wide_ref):
    out_ref[...] = outgoing_rows(state_ref, place_ref, wide_ref, slots)


def les_kernel(
    sizes, vel_ref, visc_ref, xlo_ref, xhi_ref, ylo_ref, yhi_ref, order_ref, proj_ref,
    vel_out_ref, source_ref, ext_ref, mid_ref, cells_ref,
):
    own = vel_ref.shape[2]
    own_x = vel_ref.shape[1]
    rows = ext_ref.shape[2]
    ext_ref[:, :, own:rows, :] = jnp.zeros_like(ext_ref[:, :, own:rows, :])
    ext_ref[0:3, 2 : own_x + 2, 0:own, :] = vel_ref[...]
    ext_ref[3, 2 : own_x + 2, 0:own, :] = visc_ref[...]
    ext_ref[:, 0:2, 0:own, :] = xlo_ref[...]
    ext_ref[:, own_x + 2 : own_x + 4, 0:own, :] = xhi_ref[...]
    ext_ref[:, :, own : own + 2, :] = yhi_ref[...]
    ext_ref[:, :, rows - 2 : rows, :] = ylo_ref[...]
    f, g = lax.axis_index("flow"), lax.axis_index("grp")
    edges = (f == 0, f == sizes[0] - 1, g == 0, g == sizes[1] - 1)
    les_sections(ext_ref, mid_ref, cells_ref, vel_out_ref, edges)
    source_ref[...] = source_rows(cells_ref, order_ref, proj_ref)


def home_kernel(count, arrived_ref, send_ref, mat_ref, state_ref, faces_ref):
    state = home_rows(arrived_ref[...], send_ref, count)
    state_ref[...] = state
    faces_ref[...] = faces_out(state, mat_ref)


def section_kernel(
    bz, last, state_ref, faces_ref, xl, xh, yl, yh, source_ref, own, own_low, take, mat, send_ref, *outs
):
    new = advance(
        state_ref[...], faces_ref[...], xl[...], xh[...], yl[...], yh[...],
        source_ref[...], own, own_low, take, bz,
    )
    if last:
        outs[0][...] = leaving_rows(new, send_ref)
    else:
        outs[0][...] = new
        outs[1][...] = faces_out(new, mat)


def post_kernel(returned_ref, place_ref, out_ref):
    place_out(returned_ref[...], place_ref, out_ref)


VMEM = pl.BlockSpec(memory_space=pltpu.VMEM)


def call(kernel, args, outs, scratch=()):
    return pl.pallas_call(
        kernel,
        out_shape=[jax.ShapeDtypeStruct(s, F32) for s in outs],
        in_specs=[VMEM] * len(args),
        out_specs=[VMEM] * len(outs),
        scratch_shapes=list(scratch),
        compiler_params=pltpu.CompilerParams(vmem_limit_bytes=40 * 2**20),
    )(*args)


def shift(low_send, high_send, axis):
    peers = lax.axis_size(axis)
    up = [(i, i + 1) for i in range(peers - 1)]
    down = [(j, i) for i, j in up]
    return lax.ppermute(high_send, axis, up), lax.ppermute(low_send, axis, down)


def body(velocity, eddy_visc, projection, acoustic_state, route_send, route_place):
    own_x, own_y, lanes = velocity.shape[1:]
    by, bz = own_y // 8, lanes // 8
    sizes = (lax.axis_size("flow"), lax.axis_size("grp"))
    cap = route_send.shape[2]
    count = acoustic_state.shape[2]
    devs = sizes[0] * sizes[1]
    slots = devs * cap
    own, own_low, send_mat, take = [jnp.asarray(m) for m in operators()]
    order = jnp.asarray(cell_order(by, bz))
    sending = route_send.reshape(1, slots)
    proj = projection.reshape(125, 64, 8).transpose(0, 2, 1).reshape(125, 512)
    proj = jnp.pad(proj, ((0, 3), (0, 0)))

    def swap(value):
        value = value.reshape(devs, cap, 512)
        value = lax.all_to_all(value, ("flow", "grp"), split_axis=0, concat_axis=0, tiled=True)
        return value.reshape(slots, 512)

    (out_rows,) = call(
        functools.partial(pre_kernel, slots), (acoustic_state, route_place), [(slots, 512)],
        [pltpu.VMEM((4, 128, count), F32)],
    )
    arrived = swap(out_rows)

    fields = jnp.concatenate([velocity, eddy_visc[None]], axis=0)
    xlo, xhi = shift(fields[:, :2], fields[:, -2:], "flow")
    low_y = jnp.concatenate([xlo[:, :, :2], fields[:, :, :2], xhi[:, :, :2]], axis=1)
    high_y = jnp.concatenate([xlo[:, :, -2:], fields[:, :, -2:], xhi[:, :, -2:]], axis=1)
    ylo, yhi = shift(low_y, high_y, "grp")
    vel_out, source = call(
        functools.partial(les_kernel, sizes),
        (velocity, eddy_visc, xlo, xhi, ylo, yhi, order, proj),
        [velocity.shape, (count, 512)],
        [
            pltpu.VMEM((4, own_x + 4, own_y + 8, lanes), F32),
            pltpu.VMEM((3, own_x + 2, own_y + 8, lanes), F32),
            pltpu.VMEM((3, own_x * 8, by * lanes), F32),
        ],
    )
    state, faces = call(
        functools.partial(home_kernel, count), (arrived, sending, send_mat),
        [(count, 512), (count, 768)],
    )
    for turn in range(AC_SECTIONS):
        xl, xh = shift(faces[:, 0:128], faces[:, 128:256], "flow")
        yl, yh = shift(faces[:bz, 256:384], faces[count - bz :, 384:512], "grp")
        last = turn == AC_SECTIONS - 1
        outs = [(slots, 512)] if last else [(count, 512), (count, 768)]
        result = call(
            functools.partial(section_kernel, bz, last),
            (state, faces, xl, xh, yl, yh, source, own, own_low, take, send_mat, sending), outs,
        )
        if not last:
            state, faces = result
    returned = swap(result[0])
    (acoustic_out,) = call(post_kernel, (returned, route_place), [acoustic_state.shape])
    return (vel_out, acoustic_out)


def solution(mesh):
    placed = (
        P(None, "flow", "grp", None),
        P("flow", "grp", None),
        P(),
        P(None, None, ("flow", "grp")),
        P(("flow", "grp"), None, None),
        P(("flow", "grp"), None),
    )
    return jax.shard_map(
        body,
        mesh=mesh,
        in_specs=placed,
        out_specs=(P(None, "flow", "grp", None), P(None, None, ("flow", "grp"))),
        check_vma=False,
    )
```

profile of v0, /device:TPU:0, one launch (start us, length us, event | category | flops | bytes accessed | tf_op | source)
XLA Modules:
  0.0 83.2 jit_solution(7797466379028685532)
XLA Ops:
  0.7 1.2 %fusion.1 = (f32[4,2,32,256]{3,2,1,0:T(8,128)S(1)}, f32[4,2,32,256]{3,2,1,0:T(8,128)S(1)}) fusion(f32[3,8,32,256]{3,2,1,0:T(8,128)} %vel_ref.1, f32[1,8,32,256]{3,2,1,0:T(8,128)} %bitcast.5), kind=kLoop, calls=%fused_computation.7 | loop fusion | flops 131072 | bytes 1572864 | tf_op jit(solution)/shard_map/concatenate | solution.py:355
  1.9 1.3 %collective-permute-start.1 = (f32[4,2,32,256]{3,2,1,0:T(8,128)S(1)}, f32[4,2,32,256]{3,2,1,0:T(8,128)S(1)}, u32[]{:S(2)}, u32[]{:S(2)}) collective-permute-start(f32[4,2,32,256]{3,2,1,0:T(8,128)S(1)} %get-tuple-element.18), channel_id=1, source_target_pairs={{4,0},{8,4},{12,8},{16,12},{20,16},{24,20},{28,24},{5,1},{9,5},{13... | collective-permute-start | bytes 786440 | tf_op jit(solution)/shard_map/ppermute | solution.py:327
  3.2 5.5 %collective-permute-start = (f32[4,2,32,256]{3,2,1,0:T(8,128)S(1)}, f32[4,2,32,256]{3,2,1,0:T(8,128)S(1)}, u32[]{:S(2)}, u32[]{:S(2)}) collective-permute-start(f32[4,2,32,256]{3,2,1,0:T(8,128)S(1)} %get-tuple-element.19), channel_id=1, source_target_pairs={{0,4},{4,8},{8,12},{12,16},{16,20},{20,24},{24,28},{1,5},{5,9},{9,... | collective-permute-start | bytes 786440 | tf_op jit(solution)/shard_map/ppermute | solution.py:327
  8.7 1.0 %copy.20.state_ref = f32[4,125,128]{2,1,0:T(8,128)S(1)} copy(f32[4,125,128]{2,0,1:T(4,128)} %param.14) | data formatting | bytes 512000 | tf_op args[3]
  9.7 0.4 shard_map.123
  10.0 0.0 copy-start.1
  10.0 0.8 reshape.27
  10.8 6.2 %all-to-all-start = ((f32[32,4,512]{2,1,0:T(4,128)}), f32[32,4,512]{2,1,0:T(4,128)S(1)}, u32[]{:S(2)}, u32[]{:S(2)}) async-start(f32[32,4,512]{2,1,0:T(4,128)} %reshape.27), calls=%async_computation | async-start | bytes 524288 | tf_op jit(solution)/shard_map/all_to_all | solution.py:346
  17.1 0.1 copy.21
  17.2 0.1 reshape.29.send_ref
  17.4 1.5 %collective-permute-done.xlo_ref = f32[4,2,32,256]{3,2,1,0:T(8,128)S(1)} collective-permute-done((f32[4,2,32,256]{3,2,1,0:T(8,128)S(1)}, f32[4,2,32,256]{3,2,1,0:T(8,128)S(1)}, u32[]{:S(2)}, u32[]{:S(2)}) %collective-permute-start) | collective-permute-done | bytes 262176 | tf_op jit(solution)/shard_map/ppermute | solution.py:327
  18.9 0.7 pad_maximum_fusion.1
  19.6 1.8 %collective-permute-start.2 = (f32[4,12,2,256]{3,2,1,0:T(2,128)}, f32[4,12,2,256]{3,2,1,0:T(2,128)S(1)}, u32[]{:S(2)}, u32[]{:S(2)}) collective-permute-start(f32[4,12,2,256]{3,2,1,0:T(2,128)} %pad_maximum_fusion.1), channel_id=1, source_target_pairs={{0,1},{1,2},{2,3},{4,5},{5,6},{6,7},{8,9},{9,10},{10,11},{12,13},{... | collective-permute-start | bytes 294920 | tf_op jit(solution)/shard_map/ppermute | solution.py:327
  21.4 0.7 fusion.3
  22.1 1.3 %collective-permute-start.3 = (f32[4,12,2,256]{3,2,1,0:T(2,128)}, f32[4,12,2,256]{3,2,1,0:T(2,128)S(1)}, u32[]{:S(2)}, u32[]{:S(2)}) collective-permute-start(f32[4,12,2,256]{3,2,1,0:T(2,128)} %fusion.3), channel_id=1, source_target_pairs={{1,0},{2,1},{3,2},{5,4},{6,5},{7,6},{9,8},{10,9},{11,10},{13,12},{... | collective-permute-start | bytes 294920 | tf_op jit(solution)/shard_map/ppermute | solution.py:327
  23.4 4.3 %all-to-all-done = f32[32,4,512]{2,1,0:T(4,128)S(1)} async-done(((f32[32,4,512]{2,1,0:T(4,128)}), f32[32,4,512]{2,1,0:T(4,128)S(1)}, u32[]{:S(2)}, u32[]{:S(2)}) %all-to-all-start) | async-done | bytes 262176 | tf_op jit(solution)/shard_map/all_to_all | solution.py:346
  27.7 0.1 reshape.28.arrived_ref
  27.8 0.7 shard_map.124
  28.4 0.7 fusion.8
  29.1 2.8 %collective-permute-start.4 = (f32[128,128]{1,0:T(8,128)}, f32[128,128]{1,0:T(8,128)S(1)}, u32[]{:S(2)}, u32[]{:S(2)}) collective-permute-start(f32[128,128]{1,0:T(8,128)} %get-tuple-element.27), channel_id=1, source_target_pairs={{0,4},{4,8},{8,12},{12,16},{16,20},{20,24},{24,28},{1,5},{5,9},{9,... | collective-permute-start | bytes 196616 | tf_op jit(solution)/shard_map/ppermute | solution.py:327
  31.9 1.3 %collective-permute-start.5 = (f32[128,128]{1,0:T(8,128)}, f32[128,128]{1,0:T(8,128)S(1)}, u32[]{:S(2)}, u32[]{:S(2)}) collective-permute-start(f32[128,128]{1,0:T(8,128)} %get-tuple-element.26), channel_id=1, source_target_pairs={{4,0},{8,4},{12,8},{16,12},{20,16},{24,20},{28,24},{5,1},{9,5},{13... | collective-permute-start | bytes 196616 | tf_op jit(solution)/shard_map/ppermute | solution.py:327
  33.2 2.1 %collective-permute-start.6 = (f32[32,128]{1,0:T(8,128)S(1)}, f32[32,128]{1,0:T(8,128)S(1)}, u32[]{:S(2)}, u32[]{:S(2)}) collective-permute-start(f32[32,128]{1,0:T(8,128)S(1)} %get-tuple-element.25), channel_id=1, source_target_pairs={{0,1},{1,2},{2,3},{4,5},{5,6},{6,7},{8,9},{9,10},{10,11},{12,13},{... | collective-permute-start | bytes 49160 | tf_op jit(solution)/shard_map/ppermute | solution.py:327
  35.3 1.3 %collective-permute-start.7 = (f32[32,128]{1,0:T(8,128)S(1)}, f32[32,128]{1,0:T(8,128)S(1)}, u32[]{:S(2)}, u32[]{:S(2)}) collective-permute-start(f32[32,128]{1,0:T(8,128)S(1)} %get-tuple-element.24), channel_id=1, source_target_pairs={{1,0},{2,1},{3,2},{5,4},{6,5},{7,6},{9,8},{10,9},{11,10},{13,12},{... | collective-permute-start | bytes 49160 | tf_op jit(solution)/shard_map/ppermute | solution.py:327
  36.6 1.0 %copy.17 = bf16[125,512]{0,1:T(8,128)(2,1)S(1)} copy(bf16[125,512]{1,0:T(8,128)(2,1)} %param.13) | data formatting | bytes 256000 | tf_op args[2]
  37.6 0.7 copy.18
  38.3 1.0 %copy.19 = bf16[125,512]{1,0:T(8,128)(2,1)S(1)} copy(bf16[125,512]{0,1:T(8,128)(2,1)} %bitcast.8) | data formatting | bytes 256000 | tf_op jit(solution)/shard_map/reshape | solution.py:341
  39.4 0.0 collective-permute-done.3.yhi_ref
  39.4 0.0 copy-start.4
  39.4 1.7 %copy-done.4 = bf16[1024,1024]{1,0:T(8,128)(2,1)S(1)} copy-done((bf16[1024,1024]{1,0:T(8,128)(2,1)S(1)}, bf16[1024,1024]{1,0:T(8,128)(2,1)}, u32[]{:S(2)}) %copy-start.4) | copy-done | bytes 2097176
  41.0 5.5 %shard_map.122 = (f32[3,8,32,256]{3,2,1,0:T(8,128)}, f32[128,512]{1,0:T(8,128)S(1)}) custom-call(f32[3,8,32,256]{3,2,1,0:T(8,128)S(1)} %copy-done, f32[8,32,256]{2,1,0:T(8,128)S(1)} %copy-done.2, f32[4,2,32,256]{3,2,1,0:T(8,128)S(1)} %collective-permute-done.xlo_ref, f32[4,2,32,256]{3,2,1,0:T(8,128)S(1)} %collective-permute-done.1.xhi_ref, ...), custom_call_target="tpu_custom_call" | custom-call | tf_op jit(solution)/shard_map/pallas_call | solution.py:313
  46.5 0.0 collective-permute-done.6.yl
  46.5 0.0 collective-permute-done.7.yh
  46.5 0.0 collective-permute-done.5.xh
  46.6 1.1 %shard_map.125 = (f32[128,512]{1,0:T(8,128)S(1)}, f32[128,768]{1,0:T(8,128)S(1)}) custom-call(f32[128,512]{1,0:T(8,128)S(1)} %get-tuple-element.9.state_ref, f32[128,768]{1,0:T(8,128)S(1)} %get-tuple-element.10.faces_ref, f32[128,128]{1,0:T(8,128)S(1)} %collective-permute-done.4.xl, f32[128,128]{1,0:T(8,128)S(1)} %collective-permute-done.5.xh, ...), custom_call_target="tpu_custom_call" | custom-call | tf_op jit(solution)/shard_map/pallas_call | solution.py:313
  47.7 4.3 %collective-permute-start.8 = (f32[128,128]{1,0:T(8,128)S(1)}, f32[128,128]{1,0:T(8,128)S(1)}, u32[]{:S(2)}, u32[]{:S(2)}) collective-permute-start(f32[128,128]{1,0:T(8,128)S(1)} %get-tuple-element.23), channel_id=1, source_target_pairs={{0,4},{4,8},{8,12},{12,16},{16,20},{20,24},{24,28},{1,5},{5,9},{9,... | collective-permute-start | bytes 196616 | tf_op jit(solution)/shard_map/ppermute | solution.py:327
  52.0 1.3 %collective-permute-start.9 = (f32[128,128]{1,0:T(8,128)S(1)}, f32[128,128]{1,0:T(8,128)S(1)}, u32[]{:S(2)}, u32[]{:S(2)}) collective-permute-start(f32[128,128]{1,0:T(8,128)S(1)} %get-tuple-element.22), channel_id=1, source_target_pairs={{4,0},{8,4},{12,8},{16,12},{20,16},{24,20},{28,24},{5,1},{9,5},{13... | collective-permute-start | bytes 196616 | tf_op jit(solution)/shard_map/ppermute | solution.py:327
  53.3 4.6 %collective-permute-start.10 = (f32[32,128]{1,0:T(8,128)S(1)}, f32[32,128]{1,0:T(8,128)S(1)}, u32[]{:S(2)}, u32[]{:S(2)}) collective-permute-start(f32[32,128]{1,0:T(8,128)S(1)} %get-tuple-element.21), channel_id=1, source_target_pairs={{0,1},{1,2},{2,3},{4,5},{5,6},{6,7},{8,9},{9,10},{10,11},{12,13},{... | collective-permute-start | bytes 49160 | tf_op jit(solution)/shard_map/ppermute | solution.py:327
  57.8 1.3 %collective-permute-start.11 = (f32[32,128]{1,0:T(8,128)S(1)}, f32[32,128]{1,0:T(8,128)S(1)}, u32[]{:S(2)}, u32[]{:S(2)}) collective-permute-start(f32[32,128]{1,0:T(8,128)S(1)} %get-tuple-element.20), channel_id=1, source_target_pairs={{1,0},{2,1},{3,2},{5,4},{6,5},{7,6},{9,8},{10,9},{11,10},{13,12},{... | collective-permute-start | bytes 49160 | tf_op jit(solution)/shard_map/ppermute | solution.py:327
  59.1 0.0 collective-permute-done.10.yl
  59.1 3.3 %collective-permute-done.11.yh = f32[32,128]{1,0:T(8,128)S(1)} collective-permute-done((f32[32,128]{1,0:T(8,128)S(1)}, f32[32,128]{1,0:T(8,128)S(1)}, u32[]{:S(2)}, u32[]{:S(2)}) %collective-permute-start.11) | collective-permute-done | bytes 16416 | tf_op jit(solution)/shard_map/ppermute | solution.py:327
  62.4 0.0 collective-permute-done.8.xl
  62.4 0.0 collective-permute-done.9.xh
  62.4 0.9 %shard_map.126 = f32[128,512]{1,0:T(8,128)S(1)} custom-call(f32[128,512]{1,0:T(8,128)S(1)} %get-tuple-element.12.state_ref, f32[128,768]{1,0:T(8,128)S(1)} %get-tuple-element.13.faces_ref, f32[128,128]{1,0:T(8,128)S(1)} %collective-permute-done.8.xl, f32[128,128]{1,0:T(8,128)S(1)} %collective-permute-done.9.xh, f32[32,128]{1,0:T(8,128)S(1)} %collective-permute-done.10.yl, ...), custom_call_target="tpu_custom_call" | custom-call | tf_op jit(solution)/shard_map/pallas_call | solution.py:313
  63.3 0.1 reshape.30
  63.4 18.4 %all_to_all.10 = f32[32,4,512]{2,1,0:T(4,128)S(1)} all-to-all(f32[32,4,512]{2,1,0:T(4,128)S(1)} %reshape.30), channel_id=1, replica_groups=mesh['flow'=8,'grp'=4] {'flow','grp'}, dimensions={0} | all-to-all | bytes 524288 | tf_op jit(solution)/shard_map/all_to_all | solution.py:346
  81.8 0.1 reshape.31.returned_ref
  81.9 0.4 shard_map.127
  82.3 0.9 %copy.22 = f32[4,125,128]{2,0,1:T(4,128)} copy(f32[4,125,128]{2,1,0:T(8,128)S(1)} %shard_map.127) | data formatting | bytes 512000
  (25 shorter events, 0.1 us)
Async XLA Ops:
  0.6 16.4 %copy-start = (f32[3,8,32,256]{3,2,1,0:T(8,128)S(1)}, f32[3,8,32,256]{3,2,1,0:T(8,128)}, u32[]{:S(2)}) copy-start(f32[3,8,32,256]{3,2,1,0:T(8,128)} %vel_ref.1) | copy-start | bytes 2359300
  0.6 16.4 %copy-start.2 = (f32[8,32,256]{2,1,0:T(8,128)S(1)}, f32[8,32,256]{2,1,0:T(8,128)}, u32[]{:S(2)}) copy-start(f32[8,32,256]{2,1,0:T(8,128)} %visc_ref.1) | copy-start | bytes 786436
  0.7 9.0 %copy-start.7 = (s32[1,128]{1,0:T(1,128)S(1)}, s32[1,128]{1,0:T(1,128)}, u32[]{:S(2)}) copy-start(s32[1,128]{1,0:T(1,128)} %place_ref.3) | copy-start | bytes 1540
  0.7 16.5 %copy-start.8 = (s32[1,32,4]{1,2,0:T(4,128)S(1)}, s32[1,32,4]{1,2,0:T(4,128)}, u32[]{:S(2)}) copy-start(s32[1,32,4]{1,2,0:T(4,128)} %param.15) | copy-start | bytes 1540
  1.9 15.5 %collective-permute-start.1 = (f32[4,2,32,256]{3,2,1,0:T(8,128)S(1)}, f32[4,2,32,256]{3,2,1,0:T(8,128)S(1)}, u32[]{:S(2)}, u32[]{:S(2)}) collective-permute-start(f32[4,2,32,256]{3,2,1,0:T(8,128)S(1)} %get-tuple-element.18), channel_id=1, source_target_pairs={{4,0},{8,4},{12,8},{16,12},{20,16},{24,20},{28,24},{5,1},{9,5},{13... | collective-permute-start | bytes 786440 | tf_op jit(solution)/shard_map/ppermute | solution.py:327
  3.2 15.7 %collective-permute-start = (f32[4,2,32,256]{3,2,1,0:T(8,128)S(1)}, f32[4,2,32,256]{3,2,1,0:T(8,128)S(1)}, u32[]{:S(2)}, u32[]{:S(2)}) collective-permute-start(f32[4,2,32,256]{3,2,1,0:T(8,128)S(1)} %get-tuple-element.19), channel_id=1, source_target_pairs={{0,4},{4,8},{8,12},{12,16},{16,20},{20,24},{24,28},{1,5},{5,9},{9,... | collective-permute-start | bytes 786440 | tf_op jit(solution)/shard_map/ppermute | solution.py:327
  10.0 17.7 %copy-start.1 = (bf16[512,768]{1,0:T(8,128)(2,1)S(1)}, bf16[512,768]{1,0:T(8,128)(2,1)}, u32[]{:S(2)}) copy-start(bf16[512,768]{1,0:T(8,128)(2,1)} %constant.15.clone.mat_ref.mat) | copy-start | bytes 2359300
  10.8 16.8 %all-to-all-start = ((f32[32,4,512]{2,1,0:T(4,128)}), f32[32,4,512]{2,1,0:T(4,128)S(1)}, u32[]{:S(2)}, u32[]{:S(2)}) async-start(f32[32,4,512]{2,1,0:T(4,128)} %reshape.27), calls=%async_computation | async-start | bytes 524288 | tf_op jit(solution)/shard_map/all_to_all | solution.py:346
  19.6 15.7 %collective-permute-start.2 = (f32[4,12,2,256]{3,2,1,0:T(2,128)}, f32[4,12,2,256]{3,2,1,0:T(2,128)S(1)}, u32[]{:S(2)}, u32[]{:S(2)}) collective-permute-start(f32[4,12,2,256]{3,2,1,0:T(2,128)} %pad_maximum_fusion.1), channel_id=1, source_target_pairs={{0,1},{1,2},{2,3},{4,5},{5,6},{6,7},{8,9},{9,10},{10,11},{12,13},{... | collective-permute-start | bytes 294920 | tf_op jit(solution)/shard_map/ppermute | solution.py:327
  22.1 17.3 %collective-permute-start.3 = (f32[4,12,2,256]{3,2,1,0:T(2,128)}, f32[4,12,2,256]{3,2,1,0:T(2,128)S(1)}, u32[]{:S(2)}, u32[]{:S(2)}) collective-permute-start(f32[4,12,2,256]{3,2,1,0:T(2,128)} %fusion.3), channel_id=1, source_target_pairs={{1,0},{2,1},{3,2},{5,4},{6,5},{7,6},{9,8},{10,9},{11,10},{13,12},{... | collective-permute-start | bytes 294920 | tf_op jit(solution)/shard_map/ppermute | solution.py:327
  29.1 17.4 %collective-permute-start.4 = (f32[128,128]{1,0:T(8,128)}, f32[128,128]{1,0:T(8,128)S(1)}, u32[]{:S(2)}, u32[]{:S(2)}) collective-permute-start(f32[128,128]{1,0:T(8,128)} %get-tuple-element.27), channel_id=1, source_target_pairs={{0,4},{4,8},{8,12},{12,16},{16,20},{20,24},{24,28},{1,5},{5,9},{9,... | collective-permute-start | bytes 196616 | tf_op jit(solution)/shard_map/ppermute | solution.py:327
  31.9 14.7 %collective-permute-start.5 = (f32[128,128]{1,0:T(8,128)}, f32[128,128]{1,0:T(8,128)S(1)}, u32[]{:S(2)}, u32[]{:S(2)}) collective-permute-start(f32[128,128]{1,0:T(8,128)} %get-tuple-element.26), channel_id=1, source_target_pairs={{4,0},{8,4},{12,8},{16,12},{20,16},{24,20},{28,24},{5,1},{9,5},{13... | collective-permute-start | bytes 196616 | tf_op jit(solution)/shard_map/ppermute | solution.py:327
  33.2 13.3 %collective-permute-start.6 = (f32[32,128]{1,0:T(8,128)S(1)}, f32[32,128]{1,0:T(8,128)S(1)}, u32[]{:S(2)}, u32[]{:S(2)}) collective-permute-start(f32[32,128]{1,0:T(8,128)S(1)} %get-tuple-element.25), channel_id=1, source_target_pairs={{0,1},{1,2},{2,3},{4,5},{5,6},{6,7},{8,9},{9,10},{10,11},{12,13},{... | collective-permute-start | bytes 49160 | tf_op jit(solution)/shard_map/ppermute | solution.py:327
  35.3 11.2 %collective-permute-start.7 = (f32[32,128]{1,0:T(8,128)S(1)}, f32[32,128]{1,0:T(8,128)S(1)}, u32[]{:S(2)}, u32[]{:S(2)}) collective-permute-start(f32[32,128]{1,0:T(8,128)S(1)} %get-tuple-element.24), channel_id=1, source_target_pairs={{1,0},{2,1},{3,2},{5,4},{6,5},{7,6},{9,8},{10,9},{11,10},{13,12},{... | collective-permute-start | bytes 49160 | tf_op jit(solution)/shard_map/ppermute | solution.py:327
  39.3 7.2 %copy-start.3 = (bf16[768,512]{1,0:T(8,128)(2,1)S(1)}, bf16[768,512]{1,0:T(8,128)(2,1)}, u32[]{:S(2)}) copy-start(bf16[768,512]{1,0:T(8,128)(2,1)} %constant.16.clone.take) | copy-start | bytes 2359300
  39.4 1.7 %copy-start.4 = (bf16[1024,1024]{1,0:T(8,128)(2,1)S(1)}, bf16[1024,1024]{1,0:T(8,128)(2,1)}, u32[]{:S(2)}) copy-start(bf16[1024,1024]{1,0:T(8,128)(2,1)} %constant.17.clone.order_ref) | copy-start | bytes 6291460
  41.0 5.5 %copy-start.5 = (bf16[512,512]{1,0:T(8,128)(2,1)S(1)}, bf16[512,512]{1,0:T(8,128)(2,1)}, u32[]{:S(2)}) copy-start(bf16[512,512]{1,0:T(8,128)(2,1)} %constant.13.clone.own) | copy-start | bytes 1572868
  41.0 5.5 %copy-start.6 = (bf16[512,512]{1,0:T(8,128)(2,1)S(1)}, bf16[512,512]{1,0:T(8,128)(2,1)}, u32[]{:S(2)}) copy-start(bf16[512,512]{1,0:T(8,128)(2,1)} %constant.14.clone.own_low) | copy-start | bytes 1572868
  47.7 14.7 %collective-permute-start.8 = (f32[128,128]{1,0:T(8,128)S(1)}, f32[128,128]{1,0:T(8,128)S(1)}, u32[]{:S(2)}, u32[]{:S(2)}) collective-permute-start(f32[128,128]{1,0:T(8,128)S(1)} %get-tuple-element.23), channel_id=1, source_target_pairs={{0,4},{4,8},{8,12},{12,16},{16,20},{20,24},{24,28},{1,5},{5,9},{9,... | collective-permute-start | bytes 196616 | tf_op jit(solution)/shard_map/ppermute | solution.py:327
  52.0 10.5 %collective-permute-start.9 = (f32[128,128]{1,0:T(8,128)S(1)}, f32[128,128]{1,0:T(8,128)S(1)}, u32[]{:S(2)}, u32[]{:S(2)}) collective-permute-start(f32[128,128]{1,0:T(8,128)S(1)} %get-tuple-element.22), channel_id=1, source_target_pairs={{4,0},{8,4},{12,8},{16,12},{20,16},{24,20},{28,24},{5,1},{9,5},{13... | collective-permute-start | bytes 196616 | tf_op jit(solution)/shard_map/ppermute | solution.py:327
  53.3 5.9 %collective-permute-start.10 = (f32[32,128]{1,0:T(8,128)S(1)}, f32[32,128]{1,0:T(8,128)S(1)}, u32[]{:S(2)}, u32[]{:S(2)}) collective-permute-start(f32[32,128]{1,0:T(8,128)S(1)} %get-tuple-element.21), channel_id=1, source_target_pairs={{0,1},{1,2},{2,3},{4,5},{5,6},{6,7},{8,9},{9,10},{10,11},{12,13},{... | collective-permute-start | bytes 49160 | tf_op jit(solution)/shard_map/ppermute | solution.py:327
  57.8 4.6 %collective-permute-start.11 = (f32[32,128]{1,0:T(8,128)S(1)}, f32[32,128]{1,0:T(8,128)S(1)}, u32[]{:S(2)}, u32[]{:S(2)}) collective-permute-start(f32[32,128]{1,0:T(8,128)S(1)} %get-tuple-element.20), channel_id=1, source_target_pairs={{1,0},{2,1},{3,2},{5,4},{6,5},{7,6},{9,8},{10,9},{11,10},{13,12},{... | collective-permute-start | bytes 49160 | tf_op jit(solution)/shard_map/ppermute | solution.py:327
where the time goes:
time: 83.8 us; the launch traced here: 83.2 us
  starting transfers between devices  35 us (42%)
  blocking collectives  18.4 us (22%)
  waiting for transfers between devices  9.12 us (11%)
  Pallas kernels  8.89 us (11%)
  local copies, waits for them, and re-layouts  8.21 us (10%)
  other arithmetic  2.57 us (3%)
  between operations  1.04 us (1%)
    ppermute x6, starting transfers between devices, shift(): lax.ppermute(high_send, axis, up)  21 us
    all_to_all x1, blocking collectives, swap(): lax.all_to_all(value, ('flow', 'grp'), split_axis=0, concat_axis=0, tiled...  18.4 us
    pallas_call x6, Pallas kernels, call(): pl.pallas_call(kernel, out_shape=[jax.ShapeDtypeStruct(s, F32) for s in o...  8.89 us
    ppermute x6, starting transfers between devices, shift(): lax.ppermute(low_send, axis, down)  7.74 us
    all_to_all x1, starting transfers between devices, swap(): lax.all_to_all(value, ('flow', 'grp'), split_axis=0, concat_axis=0, tiled...  6.22 us
    unnamed x22, local copies, waits for them, and re-layouts  4.65 us
    all_to_all x1, waiting for transfers between devices, swap(): lax.all_to_all(value, ('flow', 'grp'), split_axis=0, concat_axis=0, tiled...  4.27 us
    ppermute x6, waiting for transfers between devices, shift(): lax.ppermute(low_send, axis, down)  3.3 us
  transfers between devices with their start and end apart: 13, of which 3 were waited for; matrix products, arithmetic and copies ran while one was open for 8% of the time, Pallas kernels for 8%

commit v1 on v0

v1 whole, which is shorter than its diff:
```python
import functools
import math

import jax
import jax.numpy as jnp
import ml_dtypes
import numpy as np
from jax import lax
from jax.experimental import pallas as pl
from jax.experimental.pallas import tpu as pltpu
from jax.sharding import PartitionSpec as P

LES_SECTIONS = 2
AC_SECTIONS = 2

TIME_STEP_LES = 0.15
TIME_STEP_ACOUSTIC = 0.02
GEOMETRY = 2.0
LIFT_FACTOR = 20.0
F32 = jnp.float32
BF16 = jnp.bfloat16


def gll_derivative():
    gll_nodes = np.array([-1.0, -math.sqrt(3.0 / 7.0), 0.0, math.sqrt(3.0 / 7.0), 1.0])
    bary_weights = np.array(
        [
            1.0
            / np.prod([gll_nodes[first] - gll_nodes[other] for other in range(5) if other != first])
            for first in range(5)
        ]
    )
    matrix = np.zeros((5, 5))
    for row_id in range(5):
        for col_id in range(5):
            if row_id != col_id:
                matrix[row_id, col_id] = (
                    bary_weights[col_id]
                    / bary_weights[row_id]
                    / (gll_nodes[row_id] - gll_nodes[col_id])
                )
    for row_id in range(5):
        matrix[row_id, row_id] = -matrix[row_id].sum()
    return matrix


def operators():
    dmat = gll_derivative()
    eye = np.eye(5)
    kron = lambda a, b, c: np.kron(np.kron(a, b), c)
    derivs = [kron(dmat, eye, eye), kron(eye, dmat, eye), kron(eye, eye, dmat)]
    own = np.zeros((512, 512))
    for k in range(3):
        u = 128 * (k + 1)
        own[u : u + 125, 0:125] += -GEOMETRY * derivs[k].T
        own[0:125, u : u + 125] += -GEOMETRY * derivs[k].T
    half = 0.5 * LIFT_FACTOR
    send = np.zeros((512, 768))
    take = np.zeros((768, 512))
    for d in range(3):
        pos = [np.arange(125) // 25, np.arange(125) // 5 % 5, np.arange(125) % 5][d]
        others = [k for k in range(3) if k != d]
        faces = {-1: np.where(pos == 0)[0], 1: np.where(pos == 4)[0]}
        for sign in (-1, 1):
            for n in faces[sign]:
                own[128 * (d + 1) + n, n] += half * sign
                own[n, 128 * (d + 1) + n] += half * sign
                for c in range(4):
                    own[128 * c + n, 128 * c + n] -= half
            base = (2 * d + (sign + 1) // 2) * 128
            for i, n in enumerate(faces[sign]):
                send[n, base + i] = 1.0
                send[128 * (d + 1) + n, base + i] = sign
                for t, k in enumerate(others):
                    send[128 * (k + 1) + n, base + 25 * (t + 1) + i] = 1.0
            for i, n in enumerate(faces[sign]):
                take[base + i, n] = 1.0
                take[base + i, 128 * (d + 1) + n] = -sign
                for t, k in enumerate(others):
                    take[base + 25 * (t + 1) + i, 128 * (k + 1) + n] = 1.0
    own = own * TIME_STEP_ACOUSTIC
    high = own.astype(ml_dtypes.bfloat16)
    low = (own - high.astype(np.float64)).astype(ml_dtypes.bfloat16)
    return high, low, send.astype(ml_dtypes.bfloat16), take.astype(ml_dtypes.bfloat16)


def cell_order(by, bz):
    count = by * bz * 8
    ids = np.arange(count)
    matrix = np.zeros((count, count), ml_dtypes.bfloat16)
    matrix[ids, (ids % 8) * (by * bz) + ids // 8] = 1
    return matrix


def pieces(value, count):
    out = []
    for _ in range(count):
        part = value.astype(BF16)
        out.append(part)
        value = value - part.astype(F32)
    return out


def mm(a, b):
    return jnp.dot(a, b, preferred_element_type=F32)


def pick(onehot, value):
    a, b, c = pieces(value, 3)
    return (mm(onehot, a) + mm(onehot, b)) + mm(onehot, c)


def slot_matrix(place_ref, devs, cap):
    count = place_ref.shape[1]
    place = place_ref[...]
    row = (place // cap) * 8 + place % cap
    ids = lax.broadcasted_iota(jnp.int32, (devs * 8, count), 0)
    return [jnp.where(ids == row + q * cap, 1.0, 0.0) for q in range(8 // cap)]


def home_matrix(send_ref, count, cap):
    slots = send_ref.shape[1]
    ids = lax.broadcasted_iota(jnp.int32, (count, slots), 0)
    part = (lax.broadcasted_iota(jnp.int32, (count, slots), 1) % 8) // cap
    hit = ids == send_ref[...]
    return [jnp.where(jnp.logical_and(hit, part == q), 1.0, 0.0) for q in range(8 // cap)]


def spread(mats, rows):
    width = rows.shape[1] // len(mats)
    stacked = jnp.concatenate([rows[:, q * width : (q + 1) * width] for q in range(len(mats))], axis=0)
    return pick(jnp.concatenate(mats, axis=1).astype(BF16), stacked)


def gather(mats, rows):
    count = mats[0].shape[0]
    both = pick(jnp.concatenate(mats, axis=0).astype(BF16), rows)
    return jnp.concatenate([both[q * count : (q + 1) * count] for q in range(len(mats))], axis=1)


def faces_out(state, mat):
    high, low = pieces(state, 2)
    return mm(high, mat) + mm(low, mat)


def advance(state, faces, x_low, x_high, y_low, y_high, source, own_mat, own_low, take_mat, bz):
    count = state.shape[0]
    rows = lax.broadcasted_iota(jnp.int32, (count, 128), 0)
    part = lambda i: faces[:, 128 * i : 128 * (i + 1)]
    from_low_y = jnp.concatenate([y_low, part(3)[: count - bz]], axis=0)
    from_high_y = jnp.concatenate([part(2)[bz:], y_high], axis=0)
    from_low_z = jnp.where(rows % bz == 0, 0.0, pltpu.roll(part(5), 1, 0))
    from_high_z = jnp.where(rows % bz == bz - 1, 0.0, pltpu.roll(part(4), count - 1, 0))
    incoming = jnp.concatenate(
        [x_low, x_high, from_low_y, from_high_y, from_low_z, from_high_z], axis=1
    )
    high, low = pieces(state, 2)
    mat = own_mat
    change = mm(high, mat) + (mm(high, own_low) + mm(low, mat))
    in_high, in_low = pieces(incoming, 2)
    lift = mm(in_high, take_mat) + mm(in_low, take_mat)
    scale = TIME_STEP_ACOUSTIC * 0.5 * LIFT_FACTOR
    return state + (change + scale * lift) - TIME_STEP_ACOUSTIC * source


def around(field):
    mid = field[1]
    rows, lanes = mid.shape
    lane = lax.broadcasted_iota(jnp.int32, (rows, lanes), 1)
    return (
        field[0],
        field[2],
        pltpu.roll(mid, 1, 0),
        pltpu.roll(mid, rows - 1, 0),
        jnp.where(lane == 0, 0.0, pltpu.roll(mid, 1, 1)),
        jnp.where(lane == lanes - 1, 0.0, pltpu.roll(mid, lanes - 1, 1)),
    )


def lamb_plane(near, mids):
    d = lambda c, axis: 0.5 * (near[c][2 * axis + 1] - near[c][2 * axis])
    vort_x = d(2, 1) - d(1, 2)
    vort_y = d(0, 2) - d(2, 0)
    vort_z = d(1, 0) - d(0, 1)
    return [
        vort_y * mids[2] - vort_z * mids[1],
        vort_z * mids[0] - vort_x * mids[2],
        vort_x * mids[1] - vort_y * mids[0],
    ]


def les_plane(vel, visc):
    weights = [0.5 * (visc[1] + w) for w in around(visc)]
    mids = [f[1] for f in vel]
    near = [around(f) for f in vel]
    lamb = lamb_plane(near, mids)
    new = []
    for c in range(3):
        total = weights[0] * (near[c][0] - mids[c])
        for i in range(1, 6):
            total = total + weights[i] * (near[c][i] - mids[c])
        new.append(mids[c] + TIME_STEP_LES * (total - lamb[c]))
    return new


def les_first(ext_ref, mid_ref, own_rows, edges):
    planes, rows, lanes = ext_ref.shape[1:]
    at_x0, at_x1, at_y0, at_y1 = edges
    row = lax.broadcasted_iota(jnp.int32, (rows, lanes), 0)
    below = jnp.where(at_y0, own_rows + 4, rows)
    above = jnp.where(at_y1, own_rows, own_rows + 4)
    inside = jnp.where(
        jnp.logical_or(row < above, jnp.logical_and(row >= own_rows + 4, row < below)), 1.0, 0.0
    )

    def step(i, carry):
        vel = [[ext_ref[c, i + j] for j in range(3)] for c in range(3)]
        new = les_plane(vel, [ext_ref[3, i + j] for j in range(3)])
        outside = jnp.logical_or(
            jnp.logical_and(at_x0, i == 0), jnp.logical_and(at_x1, i == planes - 3)
        )
        keep = inside * jnp.where(outside, 0.0, 1.0)
        for c in range(3):
            mid_ref[c, i] = new[c] * keep
        return carry

    lax.fori_loop(0, planes - 2, step, 0)


def les_lamb(mid_ref, cells_ref, own_rows):
    planes, rows, lanes = mid_ref.shape[1:]

    def step(i, carry):
        vel = [[mid_ref[c, i + j] for j in range(3)] for c in range(3)]
        lamb = lamb_plane([around(f) for f in vel], [f[1] for f in vel])
        at = pl.ds(pl.multiple_of(i * 8, 8), 8)
        for c in range(3):
            for ey in range(own_rows // 8):
                cells_ref[c, at, ey * lanes : (ey + 1) * lanes] = lamb[c][8 * ey : 8 * ey + 8]
        return carry

    lax.fori_loop(0, planes - 2, step, 0)


def les_second(ext_ref, mid_ref, vel_out_ref):
    own_rows = vel_out_ref.shape[2]

    def step(i, carry):
        vel = [[mid_ref[c, i + j] for j in range(3)] for c in range(3)]
        new = les_plane(vel, [ext_ref[3, i + 1 + j] for j in range(3)])
        for c in range(3):
            vel_out_ref[c, i] = new[c][0:own_rows]
        return carry

    lax.fori_loop(0, vel_out_ref.shape[1], step, 0)


def source_rows(cells_ref, order, proj):
    count = order.shape[0] // 8
    parts = [jnp.zeros((count, 128), F32)]
    for c in range(3):
        moved = mm(cells_ref[c].astype(BF16), order).astype(BF16)
        cells = jnp.concatenate([moved[:, count * k : count * (k + 1)] for k in range(8)], axis=0)
        parts.append(mm(proj, cells).T)
    return jnp.concatenate(parts, axis=1)


MESH = pl.DeviceIdType.MESH


def kernel(
    sizes, cap, bz,
    vel_ref, visc_ref, state_ref, place_ref, send_ref, proj_ref, *refs,
):
    consts, refs = refs[:6], refs[6:]
    (vel_out_ref, out_ref), refs = refs[:2], refs[2:]
    local, refs = refs[:6], refs[6:]
    (
        ext, mid, cells, wide, proj_rows, out_buf, in_buf, back_out, back_in,
        stage_out, stage_in, fx_out, fx_in, fy_out, fy_in,
        local_sem, a2a_send, a2a_recv, halo_send, halo_recv, face_send, face_recv,
    ) = refs
    n_flow, n_grp = sizes
    devs = n_flow * n_grp
    f, g = lax.axis_index("flow"), lax.axis_index("grp")
    me = f * n_grp + g
    edges = (f == 0, f == n_flow - 1, g == 0, g == n_grp - 1)
    own_x, own = vel_ref.shape[1:3]
    rows = ext.shape[2]
    count = place_ref.shape[1]

    barrier = pltpu.get_barrier_semaphore()

    def greet(i, carry):
        peer = lax.rem(me + i, devs)
        pl.semaphore_signal(
            barrier, inc=1, device_id=(peer // n_grp, lax.rem(peer, n_grp)), device_id_type=MESH
        )
        return carry

    lax.fori_loop(1, devs, greet, 0)

    loads = [pltpu.make_async_copy(c, l, local_sem.at[i]) for i, (c, l) in enumerate(zip(consts, local))]
    for load in loads:
        load.start()

    ext[:, :, own:rows, :] = jnp.zeros_like(ext[:, :, own:rows, :])
    ext[0:3, 2 : own_x + 2, 0:own, :] = vel_ref[...]
    ext[3, 2 : own_x + 2, 0:own, :] = visc_ref[...]

    lower = {"flow": (f - 1, g), "grp": (f, g - 1)}
    upper = {"flow": (f + 1, g), "grp": (f, g + 1)}
    has = {"flow": (f > 0, f < n_flow - 1), "grp": (g > 0, g < n_grp - 1)}

    def pair(axis, down_src, down_dst, up_src, up_dst, send, recv, s):
        down = pltpu.make_async_remote_copy(
            down_src, down_dst, send(s), recv(s), device_id=lower[axis], device_id_type=MESH
        )
        up = pltpu.make_async_remote_copy(
            up_src, up_dst, send(s + 1), recv(s + 1), device_id=upper[axis], device_id_type=MESH
        )
        has_low, has_up = has[axis]

        def start():
            pl.when(has_low)(down.start)
            pl.when(has_up)(up.start)

        def arrive():
            pl.when(has_up)(down.wait_recv)
            pl.when(has_low)(up.wait_recv)

        def sent():
            pl.when(has_low)(down.wait_send)
            pl.when(has_up)(up.wait_send)

        return start, arrive, sent

    def at_halo(ref):
        return lambda s: ref.at[s]

    x_halo = pair(
        "flow",
        ext.at[:, 2:4, 0:own, :], ext.at[:, own_x + 2 : own_x + 4, 0:own, :],
        ext.at[:, own_x : own_x + 2, 0:own, :], ext.at[:, 0:2, 0:own, :],
        at_halo(halo_send), at_halo(halo_recv), 0,
    )
    y_halo = pair(
        "grp", stage_out.at[0], stage_in.at[1], stage_out.at[1], stage_in.at[0],
        at_halo(halo_send), at_halo(halo_recv), 2,
    )
    x_face, y_face = [], []
    for t in range(AC_SECTIONS):
        sems = (lambda s, t=t: face_send.at[t, s], lambda s, t=t: face_recv.at[t, s])
        x_face.append(pair(
            "flow", fx_out.at[t, 0], fx_in.at[t, 1], fx_out.at[t, 1], fx_in.at[t, 0], *sems, 0
        ))
        y_face.append(pair(
            "grp", fy_out.at[t, 0], fy_in.at[t, 1], fy_out.at[t, 1], fy_in.at[t, 0], *sems, 2
        ))

    @pl.when(edges[0])
    def _():
        ext[:, 0:2, 0:own, :] = jnp.zeros_like(ext[:, 0:2, 0:own, :])
        fx_in[:, 0] = jnp.zeros_like(fx_in[:, 0])

    @pl.when(edges[1])
    def _():
        ext[:, own_x + 2 :, 0:own, :] = jnp.zeros_like(ext[:, own_x + 2 :, 0:own, :])
        fx_in[:, 1] = jnp.zeros_like(fx_in[:, 1])

    @pl.when(edges[2])
    def _():
        stage_in[0] = jnp.zeros_like(stage_in[0])
        fy_in[:, 0] = jnp.zeros_like(fy_in[:, 0])

    @pl.when(edges[3])
    def _():
        stage_in[1] = jnp.zeros_like(stage_in[1])
        fy_in[:, 1] = jnp.zeros_like(fy_in[:, 1])

    pl.semaphore_wait(barrier, devs - 1)
    x_halo[0]()

    def scatter(src, dst, s):
        def step(i, carry):
            peer = lax.rem(me + i, devs)
            pltpu.make_async_remote_copy(
                src.at[peer], dst.at[me], a2a_send.at[s], a2a_recv.at[s],
                device_id=(peer // n_grp, lax.rem(peer, n_grp)), device_id_type=MESH,
            ).start()
            return carry

        lax.fori_loop(1, devs, step, 0)
        dst[me] = src[me]

    def settle(src, dst, s):
        peer = lax.rem(me + 1, devs)
        return pltpu.make_async_remote_copy(
            src.at[0 : devs - 1], dst.at[0 : devs - 1], a2a_send.at[s], a2a_recv.at[s],
            device_id=(peer // n_grp, lax.rem(peer, n_grp)), device_id_type=MESH,
        )

    wide[...] = jnp.zeros_like(wide)
    for c in range(4):
        wide[c, 0:125, :] = state_ref[c]
    owned = jnp.concatenate([wide[c].T for c in range(4)], axis=1)
    by_place = slot_matrix(place_ref, devs, cap)
    out_buf[...] = spread(by_place, owned).reshape(out_buf.shape)
    scatter(out_buf, in_buf, 0)

    x_halo[1]()
    for c in range(4):
        stage_out[0, :, 2 * c : 2 * c + 2, :] = ext[c, :, 0:2, :]
        stage_out[1, :, 2 * c : 2 * c + 2, :] = ext[c, :, own - 2 : own, :]
    y_halo[0]()

    for load in loads:
        load.wait()
    order, reorder, own_mat, own_low, send_mat, take_mat = local
    proj_rows[...] = jnp.zeros_like(proj_rows)
    proj_rows[0:125, :] = mm(proj_ref[...], reorder[...])

    def send_faces(state, t):
        faces = faces_out(state, send_mat[...])
        fx_out[t, 0] = faces[:, 0:128]
        fx_out[t, 1] = faces[:, 128:256]
        fy_out[t, 0] = faces[:bz, 256:384]
        fy_out[t, 1] = faces[count - bz :, 384:512]
        x_face[t][0]()
        y_face[t][0]()
        return faces

    def take_faces(state, faces, source, t):
        x_face[t][1]()
        y_face[t][1]()
        return advance(
            state, faces, fx_in[t, 0], fx_in[t, 1], fy_in[t, 0], fy_in[t, 1], source,
            own_mat[...], own_low[...], take_mat[...], bz,
        )

    def les_ready():
        y_halo[1]()
        for c in range(4):
            ext[c, :, own : own + 2, :] = stage_in[1, :, 2 * c : 2 * c + 2, :]
            ext[c, :, rows - 2 : rows, :] = stage_in[0, :, 2 * c : 2 * c + 2, :]

    les_ready()
    les_first(ext, mid, own, edges)
    settle(out_buf, in_buf, 0).wait_recv()
    to_home = home_matrix(send_ref, count, cap)
    state = gather(to_home, in_buf[...].reshape(devs * 8, in_buf.shape[2]))
    faces = send_faces(state, 0)
    les_lamb(mid, cells, own)
    source = source_rows(cells, order[...], proj_rows[...].astype(BF16))
    for t in range(AC_SECTIONS):
        state = take_faces(state, faces, source, t)
        if t < AC_SECTIONS - 1:
            faces = send_faces(state, t + 1)

    back_out[...] = spread([m.T for m in to_home], state).reshape(back_out.shape)
    scatter(back_out, back_in, 1)
    les_second(ext, mid, vel_out_ref)
    from_home = [m.T for m in by_place]
    settle(back_out, back_in, 1).wait_recv()
    final = gather(from_home, back_in[...].reshape(devs * 8, back_in.shape[2]))
    for c in range(4):
        out_ref[c] = final[:, 128 * c : 128 * (c + 1)].T[0:125]

    settle(out_buf, in_buf, 0).wait_send()
    settle(back_out, back_in, 1).wait_send()
    x_halo[2]()
    y_halo[2]()
    for t in range(AC_SECTIONS):
        x_face[t][2]()
        y_face[t][2]()


def body(velocity, eddy_visc, projection, acoustic_state, route_send, route_place):
    own_x, own_y, lanes = velocity.shape[1:]
    by, bz = own_y // 8, lanes // 8
    sizes = (lax.axis_size("flow"), lax.axis_size("grp"))
    cap = route_send.shape[2]
    count = acoustic_state.shape[2]
    devs = sizes[0] * sizes[1]
    width = 512 * cap // 8
    ids = np.arange(512)
    reorder = np.zeros((512, 512), ml_dtypes.bfloat16)
    reorder[ids, (ids % 8) * 64 + ids // 8] = 1
    consts = [jnp.asarray(m) for m in (cell_order(by, bz), reorder, *operators())]
    sending = jnp.broadcast_to(route_send.reshape(devs, 1, cap), (devs, 8 // cap, cap))
    args = (velocity, eddy_visc, acoustic_state, route_place, sending.reshape(1, devs * 8), projection)
    vmem = pl.BlockSpec(memory_space=pltpu.VMEM)
    dma = pltpu.SemaphoreType.DMA
    chunk = pltpu.VMEM((devs, 8, width), F32)
    return tuple(pl.pallas_call(
        functools.partial(kernel, sizes, cap, bz),
        out_shape=[
            jax.ShapeDtypeStruct(velocity.shape, F32),
            jax.ShapeDtypeStruct(acoustic_state.shape, F32),
        ],
        in_specs=[vmem] * len(args) + [pl.BlockSpec(memory_space=pl.ANY)] * len(consts),
        out_specs=[vmem] * 2,
        scratch_shapes=[pltpu.VMEM(c.shape, BF16) for c in consts] + [
            pltpu.VMEM((4, own_x + 4, own_y + 8, lanes), F32),
            pltpu.VMEM((3, own_x + 2, own_y + 8, lanes), F32),
            pltpu.VMEM((3, own_x * 8, by * lanes), F32),
            pltpu.VMEM((4, 128, count), F32),
            pltpu.VMEM((128, 512), F32),
            chunk, chunk, chunk, chunk,
            pltpu.VMEM((2, own_x + 4, 8, lanes), F32),
            pltpu.VMEM((2, own_x + 4, 8, lanes), F32),
            pltpu.VMEM((AC_SECTIONS, 2, count, 128), F32),
            pltpu.VMEM((AC_SECTIONS, 2, count, 128), F32),
            pltpu.VMEM((AC_SECTIONS, 2, bz, 128), F32),
            pltpu.VMEM((AC_SECTIONS, 2, bz, 128), F32),
            dma((len(consts),)), dma((2,)), dma((2,)), dma((4,)), dma((4,)),
            dma((AC_SECTIONS, 4)), dma((AC_SECTIONS, 4)),
        ],
        compiler_params=pltpu.CompilerParams(
            collective_id=0, has_side_effects=True, vmem_limit_bytes=56 * 2**20
        ),
    )(*args, *consts))


def solution(mesh):
    placed = (
        P(None, "flow", "grp", None),
        P("flow", "grp", None),
        P(),
        P(None, None, ("flow", "grp")),
        P(("flow", "grp"), None, None),
        P(("flow", "grp"), None),
    )
    return jax.shard_map(
        body,
        mesh=mesh,
        in_specs=placed,
        out_specs=(P(None, "flow", "grp", None), P(None, None, ("flow", "grp"))),
        check_vma=False,
    )
```

time: 83.8 us -> 53.7 us (0.64)
  Pallas kernels: 8.89 us -> 45.6 us
  starting transfers between devices: 35 us -> 0 us
  blocking collectives: 18.4 us -> 0 us
  waiting for transfers between devices: 9.12 us -> 0 us
  other arithmetic: 2.57 us -> 0 us
  local copies, waits for them, and re-layouts: 8.21 us -> 7.02 us
    pallas_call x6 -> x1, Pallas kernels: 8.89 us -> 45.6 us  [body(): pl.pallas_call(functools.partial(kernel, sizes, cap, bz), out_shape=[jax....]
    ppermute x12 -> x0, starting transfers between devices: 28.7 us -> none  [the longest x6 21 us: shift(): lax.ppermute(high_send, axis, up)]
    all_to_all x1 -> x0, blocking collectives: 18.4 us -> none  [swap(): lax.all_to_all(value, ('flow', 'grp'), split_axis=0, concat_axis=0, tiled...]
    all_to_all x1 -> x0, starting transfers between devices: 6.22 us -> none  [swap(): lax.all_to_all(value, ('flow', 'grp'), split_axis=0, concat_axis=0, tiled...]
    ppermute x12 -> x0, waiting for transfers between devices: 4.85 us -> none  [the longest x6 3.3 us: shift(): lax.ppermute(low_send, axis, down)]
    all_to_all x1 -> x0, waiting for transfers between devices: 4.27 us -> none  [swap(): lax.all_to_all(value, ('flow', 'grp'), split_axis=0, concat_axis=0, tiled...]
    concatenate x4 -> x0, other arithmetic: 2.57 us -> none  [the longest x2 1.21 us: body(): fields = jnp.concatenate([velocity, eddy_visc[None]], axis=0)]
    pallas_call x0 -> x1, local copies, waits for them, and re-layouts: none -> 1.81 us  [body(): pl.pallas_call(functools.partial(kernel, sizes, cap, bz), out_shape=[jax....]
  transfers between devices with their start and end apart: 13 -> 0, of which waited for: 3 -> 0; matrix products, arithmetic and copies ran while one was open for 8% -> 0% of each run, Pallas kernels for 8% -> 0%
where the time goes in v1:
time: 53.7 us; the launch traced here: 53.2 us
  Pallas kernels  45.6 us (85%)
  local copies, waits for them, and re-layouts  7.02 us (13%)
  between operations  0.64 us (1%)
    pallas_call x1, Pallas kernels, body(): pl.pallas_call(functools.partial(kernel, sizes, cap, bz), out_shape=[jax....  45.6 us
    unnamed x2, local copies, waits for them, and re-layouts  3.76 us
    pallas_call x1, local copies, waits for them, and re-layouts, body(): pl.pallas_call(functools.partial(kernel, sizes, cap, bz), out_shape=[jax....  1.81 us

profile of v1, /device:TPU:0, one launch (start us, length us, event | category | flops | bytes accessed | tf_op | source)
XLA Modules:
  0.0 53.2 jit_solution(11841314341484022800)
XLA Ops:
  0.6 0.8 %copy.17 = s32[32,4]{1,0:T(8,128)S(1)} copy(s32[32,4]{0,1:T(4,128)} %bitcast.1) | data formatting | bytes 1024 | tf_op jit(solution)/shard_map/broadcast_in_dim | solution.py:490
  1.4 0.7 %reshape.9.send_ref = s32[1,256]{1,0:T(1,128)} reshape(s32[32,2,4]{2,1,0:T(2,128)S(1)} %broadcast_in_dim.8) | data formatting | bytes 2048 | tf_op jit(solution)/shard_map/reshape | solution.py:491
  2.1 1.7 %copy.18.state_ref = f32[4,125,128]{2,1,0:T(8,128)} copy(f32[4,125,128]{2,0,1:T(4,128)} %param.15) | data formatting | bytes 512000 | tf_op args[3]
  3.8 45.6 %shard_map.131 = (f32[3,8,32,256]{3,2,1,0:T(8,128)}, f32[4,125,128]{2,1,0:T(8,128)}) custom-call(f32[3,8,32,256]{3,2,1,0:T(8,128)} %vel_ref.1, f32[8,32,256]{2,1,0:T(8,128)} %visc_ref.1, f32[4,125,128]{2,1,0:T(8,128)} %copy.18.state_ref, s32[1,128]{1,0:T(1,128)} %place_ref.1, s32[1,256]{1,0:T(1,128)} %reshape.9.send_ref, bf16[125,512]{1,0:T(8,128)(2,1)} %proj_ref.1, ...), custom_call_target="tpu_custom_call" | custom-call | tf_op jit(solution)/shard_map/pallas_call | solution.py:495
  49.3 1.8 %copy.19 = f32[4,125,128]{2,0,1:T(4,128)} copy(f32[4,125,128]{2,1,0:T(8,128)} %get-tuple-element.5) | data formatting | bytes 512000 | tf_op jit(solution)/shard_map/pallas_call | solution.py:495
  51.1 2.1 %copy.21 = f32[3,8,32,256]{3,2,1,0:T(8,128)} copy(f32[3,8,32,256]{3,2,1,0:T(8,128)} %get-tuple-element.8) | data formatting | bytes 1572864
  (1 shorter events, 0.0 us)

commit v2 on v1

--- a/solution.py
+++ b/solution.py
@@ -118,11 +118,17 @@
     return [jnp.where(ids == row + q * cap, 1.0, 0.0) for q in range(8 // cap)]
 
 
-def home_matrix(send_ref, count, cap):
-    slots = send_ref.shape[1]
-    ids = lax.broadcasted_iota(jnp.int32, (count, slots), 0)
-    part = (lax.broadcasted_iota(jnp.int32, (count, slots), 1) % 8) // cap
-    hit = ids == send_ref[...]
+def home_matrix(send_ref, count):
+    cap, devs = send_ref.shape
+    slots = devs * 8
+    wide = lambda shape, dim: lax.broadcasted_iota(jnp.int32, shape, dim)
+    own = wide((devs, slots), 1) // 8 == wide((devs, slots), 0)
+    each = mm(send_ref[...].astype(F32).astype(BF16), jnp.where(own, 1.0, 0.0).astype(BF16))
+    kept = wide((cap, slots), 1) % cap == wide((cap, slots), 0)
+    sending = jnp.sum(jnp.where(kept, each, 0.0), axis=0, keepdims=True).astype(jnp.int32)
+    ids = wide((count, slots), 0)
+    part = (wide((count, slots), 1) % 8) // cap
+    hit = ids == sending
     return [jnp.where(jnp.logical_and(hit, part == q), 1.0, 0.0) for q in range(8 // cap)]
 
 
@@ -402,7 +408,7 @@
 
     wide[...] = jnp.zeros_like(wide)
     for c in range(4):
-        wide[c, 0:125, :] = state_ref[c]
+        wide[c, 0:125, :] = state_ref[:, c, :]
     owned = jnp.concatenate([wide[c].T for c in range(4)], axis=1)
     by_place = slot_matrix(place_ref, devs, cap)
     out_buf[...] = spread(by_place, owned).reshape(out_buf.shape)
@@ -447,7 +453,7 @@
     les_ready()
     les_first(ext, mid, own, edges)
     settle(out_buf, in_buf, 0).wait_recv()
-    to_home = home_matrix(send_ref, count, cap)
+    to_home = home_matrix(send_ref, count)
     state = gather(to_home, in_buf[...].reshape(devs * 8, in_buf.shape[2]))
     faces = send_faces(state, 0)
     les_lamb(mid, cells, own)
@@ -464,7 +470,7 @@
     settle(back_out, back_in, 1).wait_recv()
     final = gather(from_home, back_in[...].reshape(devs * 8, back_in.shape[2]))
     for c in range(4):
-        out_ref[c] = final[:, 128 * c : 128 * (c + 1)].T[0:125]
+        out_ref[c] = final[:, 128 * c : 128 * (c + 1)].T
 
     settle(out_buf, in_buf, 0).wait_send()
     settle(back_out, back_in, 1).wait_send()
@@ -473,6 +479,14 @@
     for t in range(AC_SECTIONS):
         x_face[t][2]()
         y_face[t][2]()
+
+
+def write_kernel(vel_ref, rows_ref, vel_out_ref, out_ref, sem):
+    copy = pltpu.make_async_copy(vel_ref, vel_out_ref, sem)
+    copy.start()
+    for c in range(4):
+        out_ref[:, c, :] = rows_ref[c, 0:125]
+    copy.wait()
 
 
 def body(velocity, eddy_visc, projection, acoustic_state, route_send, route_place):
@@ -487,16 +501,17 @@
     reorder = np.zeros((512, 512), ml_dtypes.bfloat16)
     reorder[ids, (ids % 8) * 64 + ids // 8] = 1
     consts = [jnp.asarray(m) for m in (cell_order(by, bz), reorder, *operators())]
-    sending = jnp.broadcast_to(route_send.reshape(devs, 1, cap), (devs, 8 // cap, cap))
-    args = (velocity, eddy_visc, acoustic_state, route_place, sending.reshape(1, devs * 8), projection)
+    args = (
+        velocity, eddy_visc, acoustic_state.transpose(1, 0, 2), route_place, route_send[0].T, projection
+    )
     vmem = pl.BlockSpec(memory_space=pltpu.VMEM)
     dma = pltpu.SemaphoreType.DMA
     chunk = pltpu.VMEM((devs, 8, width), F32)
-    return tuple(pl.pallas_call(
+    vel_rows, final = pl.pallas_call(
         functools.partial(kernel, sizes, cap, bz),
         out_shape=[
             jax.ShapeDtypeStruct(velocity.shape, F32),
-            jax.ShapeDtypeStruct(acoustic_state.shape, F32),
+            jax.ShapeDtypeStruct((4, 128, count), F32),
         ],
         in_specs=[vmem] * len(args) + [pl.BlockSpec(memory_space=pl.ANY)] * len(consts),
         out_specs=[vmem] * 2,
@@ -519,7 +534,18 @@
         compiler_params=pltpu.CompilerParams(
             collective_id=0, has_side_effects=True, vmem_limit_bytes=56 * 2**20
         ),
-    )(*args, *consts))
+    )(*args, *consts)
+    vel_out, nodes = pl.pallas_call(
+        write_kernel,
+        out_shape=[
+            jax.ShapeDtypeStruct(velocity.shape, F32),
+            jax.ShapeDtypeStruct((125, 4, count), F32),
+        ],
+        in_specs=[vmem, vmem],
+        out_specs=[pl.BlockSpec(memory_space=pl.ANY), vmem],
+        scratch_shapes=[pltpu.SemaphoreType.DMA],
+    )(vel_rows, final)
+    return vel_out, nodes.transpose(1, 0, 2)
 
 
 def solution(mesh):

time: 53.7 us -> 49.3 us (0.918)
  local copies, waits for them, and re-layouts: 7.02 us -> 0 us
  Pallas kernels: 45.6 us -> 48.4 us
    unnamed x2 -> x0, local copies, waits for them, and re-layouts: 3.76 us -> none
    pallas_call x0 -> x1, Pallas kernels: none -> 2.77 us  [body(): pl.pallas_call(write_kernel, out_shape=[jax.ShapeDtypeStruct(velocity.sha...]
    pallas_call x1 -> x0, local copies, waits for them, and re-layouts: 1.81 us -> none  [body(): pl.pallas_call(functools.partial(kernel, sizes, cap, bz), out_shape=[jax....]
    broadcast_in_dim x2 -> x0, local copies, waits for them, and re-layouts: 0.78 us -> none  [body(): jnp.broadcast_to(route_send.reshape(devs, 1, cap), (devs, 8 // cap, cap))]
    reshape x1 -> x0, local copies, waits for them, and re-layouts: 0.68 us -> none  [body(): sending.reshape(1, devs * 8)]
where the time goes in v2:
time: 49.3 us; the launch traced here: 49 us
  Pallas kernels  48.4 us (98%)
  between operations  0.64 us (1%)
    pallas_call x1, Pallas kernels, body(): pl.pallas_call(functools.partial(kernel, sizes, cap, bz), out_shape=[jax....  45.6 us
    pallas_call x1, Pallas kernels, body(): pl.pallas_call(write_kernel, out_shape=[jax.ShapeDtypeStruct(velocity.sha...  2.77 us

profile of v2, /device:TPU:0, one launch (start us, length us, event | category | flops | bytes accessed | tf_op | source)
XLA Modules:
  0.0 49.0 jit_solution(11123643916318611400)
XLA Ops:
  0.6 45.6 %shard_map.131 = (f32[3,8,32,256]{3,2,1,0:T(8,128)}, f32[4,128,128]{2,1,0:T(8,128)}) custom-call(f32[3,8,32,256]{3,2,1,0:T(8,128)} %vel_ref.1, f32[8,32,256]{2,1,0:T(8,128)} %visc_ref.1, f32[125,4,128]{2,1,0:T(4,128)} %bitcast.5, s32[1,128]{1,0:T(1,128)} %place_ref.1, s32[4,32]{1,0:T(4,128)} %bitcast.6, bf16[125,512]{1,0:T(8,128)(2,1)} %proj_ref.1, ...), custom_call_target="tpu_custom_call" | custom-call | tf_op jit(solution)/shard_map/pallas_call | solution.py:510
  46.2 2.8 %shard_map.132 = (f32[3,8,32,256]{3,2,1,0:T(8,128)}, f32[125,4,128]{2,1,0:T(4,128)}) custom-call(f32[3,8,32,256]{3,2,1,0:T(8,128)} %get-tuple-element.6.vel_ref, f32[4,128,128]{2,1,0:T(8,128)} %get-tuple-element.7.rows_ref), custom_call_target="tpu_custom_call" | custom-call | tf_op jit(solution)/shard_map/pallas_call | solution.py:538

commit v3 on v2

--- a/solution.py
+++ b/solution.py
@@ -209,7 +209,7 @@
     return new
 
 
-def les_first(ext_ref, mid_ref, own_rows, edges):
+def les_first(ext_ref, mid_ref, own_rows, edges, spans):
     planes, rows, lanes = ext_ref.shape[1:]
     at_x0, at_x1, at_y0, at_y1 = edges
     row = lax.broadcasted_iota(jnp.int32, (rows, lanes), 0)
@@ -230,7 +230,8 @@
             mid_ref[c, i] = new[c] * keep
         return carry
 
-    lax.fori_loop(0, planes - 2, step, 0)
+    for start, end in spans:
+        lax.fori_loop(start, end, step, 0)
 
 
 def les_lamb(mid_ref, cells_ref, own_rows):
@@ -350,10 +351,28 @@
         ext.at[:, own_x : own_x + 2, 0:own, :], ext.at[:, 0:2, 0:own, :],
         at_halo(halo_send), at_halo(halo_recv), 0,
     )
-    y_halo = pair(
-        "grp", stage_out.at[0], stage_in.at[1], stage_out.at[1], stage_in.at[0],
-        at_halo(halo_send), at_halo(halo_recv), 2,
-    )
+    y_halo, corners = [
+        pair(
+            "grp", stage_out.at[0, a:b], stage_in.at[1, a:b], stage_out.at[1, a:b], stage_in.at[0, a:b],
+            at_halo(halo_send), at_halo(halo_recv), s,
+        )
+        for a, b, s in ((0, own_x, 2), (own_x, own_x + 4, 4))
+    ]
+    own_planes = ((2, 0, own_x),)
+    end_planes = ((0, own_x, 2), (own_x + 2, own_x + 2, 2))
+
+    def stage(spans):
+        for c in range(4):
+            for at, to, n in spans:
+                stage_out[0, to : to + n, 2 * c : 2 * c + 2, :] = ext[c, at : at + n, 0:2, :]
+                stage_out[1, to : to + n, 2 * c : 2 * c + 2, :] = ext[c, at : at + n, own - 2 : own, :]
+
+    def unstage(spans):
+        for c in range(4):
+            for at, to, n in spans:
+                ext[c, at : at + n, own : own + 2, :] = stage_in[1, to : to + n, 2 * c : 2 * c + 2, :]
+                ext[c, at : at + n, rows - 2 : rows, :] = stage_in[0, to : to + n, 2 * c : 2 * c + 2, :]
+
     x_face, y_face = [], []
     for t in range(AC_SECTIONS):
         sems = (lambda s, t=t: face_send.at[t, s], lambda s, t=t: face_recv.at[t, s])
@@ -386,6 +405,8 @@
 
     pl.semaphore_wait(barrier, devs - 1)
     x_halo[0]()
+    stage(own_planes)
+    y_halo[0]()
 
     def scatter(src, dst, s):
         def step(i, carry):
@@ -414,12 +435,6 @@
     out_buf[...] = spread(by_place, owned).reshape(out_buf.shape)
     scatter(out_buf, in_buf, 0)
 
-    x_halo[1]()
-    for c in range(4):
-        stage_out[0, :, 2 * c : 2 * c + 2, :] = ext[c, :, 0:2, :]
-        stage_out[1, :, 2 * c : 2 * c + 2, :] = ext[c, :, own - 2 : own, :]
-    y_halo[0]()
-
     for load in loads:
         load.wait()
     order, reorder, own_mat, own_low, send_mat, take_mat = local
@@ -428,34 +443,38 @@
 
     def send_faces(state, t):
         faces = faces_out(state, send_mat[...])
-        fx_out[t, 0] = faces[:, 0:128]
-        fx_out[t, 1] = faces[:, 128:256]
+        fx_out[t, 0] = faces[:, 0:128].T[0:80]
+        fx_out[t, 1] = faces[:, 128:256].T[0:80]
         fy_out[t, 0] = faces[:bz, 256:384]
         fy_out[t, 1] = faces[count - bz :, 384:512]
         x_face[t][0]()
         y_face[t][0]()
         return faces
 
+    def face_rows(value):
+        return jnp.concatenate([value, jnp.zeros((48, count), F32)], axis=0).T
+
     def take_faces(state, faces, source, t):
         x_face[t][1]()
         y_face[t][1]()
         return advance(
-            state, faces, fx_in[t, 0], fx_in[t, 1], fy_in[t, 0], fy_in[t, 1], source,
+            state, faces, face_rows(fx_in[t, 0]), face_rows(fx_in[t, 1]), fy_in[t, 0], fy_in[t, 1], source,
             own_mat[...], own_low[...], take_mat[...], bz,
         )
 
-    def les_ready():
-        y_halo[1]()
-        for c in range(4):
-            ext[c, :, own : own + 2, :] = stage_in[1, :, 2 * c : 2 * c + 2, :]
-            ext[c, :, rows - 2 : rows, :] = stage_in[0, :, 2 * c : 2 * c + 2, :]
-
-    les_ready()
-    les_first(ext, mid, own, edges)
+    to_home = home_matrix(send_ref, count)
+    y_halo[1]()
+    unstage(own_planes)
+    les_first(ext, mid, own, edges, ((2, own_x),))
+    x_halo[1]()
+    stage(end_planes)
+    corners[0]()
     settle(out_buf, in_buf, 0).wait_recv()
-    to_home = home_matrix(send_ref, count)
     state = gather(to_home, in_buf[...].reshape(devs * 8, in_buf.shape[2]))
     faces = send_faces(state, 0)
+    corners[1]()
+    unstage(end_planes)
+    les_first(ext, mid, own, edges, ((0, 2), (own_x, own_x + 2)))
     les_lamb(mid, cells, own)
     source = source_rows(cells, order[...], proj_rows[...].astype(BF16))
     for t in range(AC_SECTIONS):
@@ -476,6 +495,7 @@
     settle(back_out, back_in, 1).wait_send()
     x_halo[2]()
     y_halo[2]()
+    corners[2]()
     for t in range(AC_SECTIONS):
         x_face[t][2]()
         y_face[t][2]()
@@ -524,11 +544,11 @@
             chunk, chunk, chunk, chunk,
             pltpu.VMEM((2, own_x + 4, 8, lanes), F32),
             pltpu.VMEM((2, own_x + 4, 8, lanes), F32),
-            pltpu.VMEM((AC_SECTIONS, 2, count, 128), F32),
-            pltpu.VMEM((AC_SECTIONS, 2, count, 128), F32),
+            pltpu.VMEM((AC_SECTIONS, 2, 80, count), F32),
+            pltpu.VMEM((AC_SECTIONS, 2, 80, count), F32),
             pltpu.VMEM((AC_SECTIONS, 2, bz, 128), F32),
             pltpu.VMEM((AC_SECTIONS, 2, bz, 128), F32),
-            dma((len(consts),)), dma((2,)), dma((2,)), dma((4,)), dma((4,)),
+            dma((len(consts),)), dma((2,)), dma((2,)), dma((6,)), dma((6,)),
             dma((AC_SECTIONS, 4)), dma((AC_SECTIONS, 4)),
         ],
         compiler_params=pltpu.CompilerParams(

time: 49.3 us -> 45.3 us (0.919)
  Pallas kernels: 48.4 us -> 44.5 us
    pallas_call x1, Pallas kernels: 45.6 us -> 41.7 us  [body(): pl.pallas_call(functools.partial(kernel, sizes, cap, bz), out_shape=[jax....]
where the time goes in v3:
time: 45.3 us; the launch traced here: 45.1 us
  Pallas kernels  44.5 us (98%)
  between operations  0.64 us (1%)
    pallas_call x1, Pallas kernels, body(): pl.pallas_call(functools.partial(kernel, sizes, cap, bz), out_shape=[jax....  41.7 us
    pallas_call x1, Pallas kernels, body(): pl.pallas_call(write_kernel, out_shape=[jax.ShapeDtypeStruct(velocity.sha...  2.77 us

profile of v3, /device:TPU:0, one launch (start us, length us, event | category | flops | bytes accessed | tf_op | source)
XLA Modules:
  0.0 45.1 jit_solution(5047561016662584723)
XLA Ops:
  0.6 41.7 %shard_map.131 = (f32[3,8,32,256]{3,2,1,0:T(8,128)}, f32[4,128,128]{2,1,0:T(8,128)}) custom-call(f32[3,8,32,256]{3,2,1,0:T(8,128)} %vel_ref.1, f32[8,32,256]{2,1,0:T(8,128)} %visc_ref.1, f32[125,4,128]{2,1,0:T(4,128)} %bitcast.5, s32[1,128]{1,0:T(1,128)} %place_ref.1, s32[4,32]{1,0:T(4,128)} %bitcast.6, bf16[125,512]{1,0:T(8,128)(2,1)} %proj_ref.1, ...), custom_call_target="tpu_custom_call" | custom-call | tf_op jit(solution)/shard_map/pallas_call | solution.py:530
  42.3 2.8 %shard_map.132 = (f32[3,8,32,256]{3,2,1,0:T(8,128)}, f32[125,4,128]{2,1,0:T(4,128)}) custom-call(f32[3,8,32,256]{3,2,1,0:T(8,128)} %get-tuple-element.6.vel_ref, f32[4,128,128]{2,1,0:T(8,128)} %get-tuple-element.7.rows_ref), custom_call_target="tpu_custom_call" | custom-call | tf_op jit(solution)/shard_map/pallas_call | solution.py:558

commit v4 on v3

--- a/solution.py
+++ b/solution.py
@@ -149,7 +149,12 @@
     return mm(high, mat) + mm(low, mat)
 
 
-def advance(state, faces, x_low, x_high, y_low, y_high, source, own_mat, own_low, take_mat, bz):
+def own_change(state, own_mat, own_low):
+    high, low = pieces(state, 2)
+    return mm(high, own_mat) + (mm(high, own_low) + mm(low, own_mat))
+
+
+def advance(state, faces, x_low, x_high, y_low, y_high, take_mat, bz):
     count = state.shape[0]
     rows = lax.broadcasted_iota(jnp.int32, (count, 128), 0)
     part = lambda i: faces[:, 128 * i : 128 * (i + 1)]
@@ -160,13 +165,10 @@
     incoming = jnp.concatenate(
         [x_low, x_high, from_low_y, from_high_y, from_low_z, from_high_z], axis=1
     )
-    high, low = pieces(state, 2)
-    mat = own_mat
-    change = mm(high, mat) + (mm(high, own_low) + mm(low, mat))
     in_high, in_low = pieces(incoming, 2)
     lift = mm(in_high, take_mat) + mm(in_low, take_mat)
     scale = TIME_STEP_ACOUSTIC * 0.5 * LIFT_FACTOR
-    return state + (change + scale * lift) - TIME_STEP_ACOUSTIC * source
+    return state + scale * lift
 
 
 def around(field):
@@ -455,11 +457,12 @@
         return jnp.concatenate([value, jnp.zeros((48, count), F32)], axis=0).T
 
     def take_faces(state, faces, source, t):
+        base = state + own_change(state, own_mat[...], own_low[...]) - TIME_STEP_ACOUSTIC * source
         x_face[t][1]()
         y_face[t][1]()
         return advance(
-            state, faces, face_rows(fx_in[t, 0]), face_rows(fx_in[t, 1]), fy_in[t, 0], fy_in[t, 1], source,
-            own_mat[...], own_low[...], take_mat[...], bz,
+            base, faces, face_rows(fx_in[t, 0]), face_rows(fx_in[t, 1]), fy_in[t, 0], fy_in[t, 1],
+            take_mat[...], bz,
         )
 
     to_home = home_matrix(send_ref, count)
@@ -477,12 +480,13 @@
     les_first(ext, mid, own, edges, ((0, 2), (own_x, own_x + 2)))
     les_lamb(mid, cells, own)
     source = source_rows(cells, order[...], proj_rows[...].astype(BF16))
+    leave = [m.T for m in to_home]
     for t in range(AC_SECTIONS):
         state = take_faces(state, faces, source, t)
         if t < AC_SECTIONS - 1:
             faces = send_faces(state, t + 1)
 
-    back_out[...] = spread([m.T for m in to_home], state).reshape(back_out.shape)
+    back_out[...] = spread(leave, state).reshape(back_out.shape)
     scatter(back_out, back_in, 1)
     les_second(ext, mid, vel_out_ref)
     from_home = [m.T for m in by_place]

time: 45.3 us -> 45.3 us (level)
  no operation moved by 1% of the time
where the time goes in v4:
time: 45.3 us; the launch traced here: 45.1 us
  Pallas kernels  44.4 us (98%)
  between operations  0.64 us (1%)
    pallas_call x1, Pallas kernels, body(): pl.pallas_call(functools.partial(kernel, sizes, cap, bz), out_shape=[jax....  41.7 us
    pallas_call x1, Pallas kernels, body(): pl.pallas_call(write_kernel, out_shape=[jax.ShapeDtypeStruct(velocity.sha...  2.77 us

profile of v4, /device:TPU:0, one launch (start us, length us, event | category | flops | bytes accessed | tf_op | source)
XLA Modules:
  0.0 45.1 jit_solution(15654508378213906787)
XLA Ops:
  0.6 41.7 %shard_map.131 = (f32[3,8,32,256]{3,2,1,0:T(8,128)}, f32[4,128,128]{2,1,0:T(8,128)}) custom-call(f32[3,8,32,256]{3,2,1,0:T(8,128)} %vel_ref.1, f32[8,32,256]{2,1,0:T(8,128)} %visc_ref.1, f32[125,4,128]{2,1,0:T(4,128)} %bitcast.5, s32[1,128]{1,0:T(1,128)} %place_ref.1, s32[4,32]{1,0:T(4,128)} %bitcast.6, bf16[125,512]{1,0:T(8,128)(2,1)} %proj_ref.1, ...), custom_call_target="tpu_custom_call" | custom-call | tf_op jit(solution)/shard_map/pallas_call | solution.py:534
  42.3 2.8 %shard_map.132 = (f32[3,8,32,256]{3,2,1,0:T(8,128)}, f32[125,4,128]{2,1,0:T(4,128)}) custom-call(f32[3,8,32,256]{3,2,1,0:T(8,128)} %get-tuple-element.6.vel_ref, f32[4,128,128]{2,1,0:T(8,128)} %get-tuple-element.7.rows_ref), custom_call_target="tpu_custom_call" | custom-call | tf_op jit(solution)/shard_map/pallas_call | solution.py:562
